TPU v7x, 32 devices: a whole 2x2x4 slice. The times are simulated.
32 devices in a mesh: gx: 4 (over y, x), gy: 8 (over z, core).
Axes of the slice: x: 2, y: 2, z: 4, core: 2. Of those that a mesh axis runs over, the one named last changes fastest.
Arguments:
- input_beam: float32 [2, 4096, 4096], P(None, ('gx', 'gy')), may hold values from -6 to 6
- offsets: int32 [2], replicated, may hold values from 0 to 4096
- distances: float32 [2], replicated, may hold values from 20 to 80
- screens: int32 [1, 8192, 8192], P(None, ('gx', 'gy')), may hold values from -127 to 127
- screen_scales: float32 [1, 64, 64], replicated, may hold values from 0.005 to 0.05
- last_screen: int32 [4096, 4096], P(('gx', 'gy')), may hold values from -127 to 127
- last_scales: float32 [32, 32], replicated, may hold values from 0.005 to 0.05
Outputs:
- output_beam: float32 [2, 4096, 4096], P(None, ('gx', 'gy'))
All inputs are finite; a program needn't handle non-finite values.
Results may differ from a plain program's by a relative error of at most 0.0001.
Values sent between devices are 32-bit elements; how exact they have to be, the bound alone decides.
A program may use at most 192 MiB of HBM per device.

v0:
```python
import math

import jax
import jax.numpy as jnp
from jax import lax
from jax.sharding import PartitionSpec as P


def contract(pattern, lhs_array, rhs_array):
    return jnp.einsum(
        pattern,
        lhs_array,
        rhs_array,
        precision=lax.Precision.HIGHEST,
        preferred_element_type=jnp.float32,
    )


def angle_table(length, row_count, col_count, orient):
    row_ids = jnp.arange(row_count, dtype=jnp.int32)
    col_ids = jnp.arange(col_count, dtype=jnp.int32)
    product = row_ids[:, None] * col_ids[None, :] % length
    angles = product.astype(jnp.float32) * (2.0 * math.pi / length)
    return (jnp.cos(angles), orient * jnp.sin(angles))


def transform_last(planes, orient):
    shape_all = planes.shape
    length = shape_all[-1]
    inner_size = 128
    outer_size = length // inner_size
    grouped = planes.reshape((2, -1, outer_size, inner_size))
    real_part = grouped[0]
    imag_part = grouped[1]
    cos_outer, sin_outer = angle_table(outer_size, outer_size, outer_size, orient)
    first_real = contract("bpq,pk->bkq", real_part, cos_outer) - contract(
        "bpq,pk->bkq", imag_part, sin_outer
    )
    first_imag = contract("bpq,pk->bkq", real_part, sin_outer) + contract(
        "bpq,pk->bkq", imag_part, cos_outer
    )
    twiddle_cos, twiddle_sin = angle_table(length, outer_size, inner_size, orient)
    second_real = first_real * twiddle_cos - first_imag * twiddle_sin
    second_imag = first_real * twiddle_sin + first_imag * twiddle_cos
    cos_inner, sin_inner = angle_table(inner_size, inner_size, inner_size, orient)
    out_real = contract("bkq,qm->bmk", second_real, cos_inner) - contract(
        "bkq,qm->bmk", second_imag, sin_inner
    )
    out_imag = contract("bkq,qm->bmk", second_real, sin_inner) + contract(
        "bkq,qm->bmk", second_imag, cos_inner
    )
    return jnp.stack([out_real, out_imag]).reshape(shape_all)


def move_window(blocks):
    return lax.all_to_all(blocks, ("gx", "gy"), split_axis=1, concat_axis=1, tiled=True)


def move_grid(blocks):
    return lax.all_to_all(blocks, ("gx", "gy"), split_axis=1, concat_axis=1, tiled=True)


def to_columns(planes, mover, devices_total, col_count):
    row_count = planes.shape[1]
    blocks = planes.reshape((2, row_count, devices_total, col_count)).transpose((0, 2, 3, 1))
    arrived = mover(blocks.reshape((2, devices_total, col_count * row_count)))
    arrived = arrived.reshape((2, devices_total, col_count, row_count)).transpose((0, 2, 1, 3))
    return arrived.reshape((2, col_count, devices_total * row_count))


def to_rows(planes, mover, devices_total):
    col_count = planes.shape[1]
    row_count = planes.shape[2] // devices_total
    blocks = planes.reshape((2, col_count, devices_total, row_count)).transpose((0, 2, 1, 3))
    arrived = mover(blocks.reshape((2, devices_total, col_count * row_count)))
    arrived = arrived.reshape((2, devices_total, col_count, row_count)).transpose((0, 3, 1, 2))
    return arrived.reshape((2, row_count, devices_total * col_count))


def block_scales(scales, first_row, row_count):
    block_total = scales.shape[0]
    block_ids = (first_row + jnp.arange(row_count, dtype=jnp.int32)) // 128
    onehot = (block_ids[:, None] == jnp.arange(block_total, dtype=jnp.int32)[None, :]).astype(
        jnp.float32
    )
    picked = jnp.dot(
        onehot, scales, precision=lax.Precision.HIGHEST, preferred_element_type=jnp.float32
    )
    return jnp.broadcast_to(picked[:, :, None], (row_count, block_total, 128)).reshape(
        (row_count, block_total * 128)
    )


def rotate_planes(planes, phases):
    cosine = jnp.cos(phases)
    sine = jnp.sin(phases)
    return jnp.stack([planes[0] * cosine - planes[1] * sine, planes[0] * sine + planes[1] * cosine])


def signed_index(indices, length):
    return jnp.where(indices < length // 2, indices, indices - length)


def body(input_beam, offsets, distances, screens, screen_scales, last_screen, last_scales):
    devices_total = lax.axis_size(("gx", "gy"))
    position = lax.axis_index(("gx", "gy"))
    grid_size = screens.shape[2]
    window_size = input_beam.shape[2]
    beam_rows = input_beam.shape[1]
    grid_rows = screens.shape[1]
    col_count = grid_size // devices_total
    step_total = distances.shape[0]
    zero_index = jnp.zeros((), jnp.int32)
    phase_coef = (2.0 * math.pi / grid_size) ** 2
    col_ids = signed_index(position * col_count + jnp.arange(col_count, dtype=jnp.int32), grid_size)
    row_ids = signed_index(jnp.arange(grid_size, dtype=jnp.int32), grid_size)
    squared = (col_ids[:, None] * col_ids[:, None] + row_ids[None, :] * row_ids[None, :]).astype(
        jnp.float32
    )
    crop_start = (grid_size - window_size) // 2
    scaling = 1.0 / grid_size
    beam_field = input_beam
    for layer_index in range(step_total):
        if layer_index == 0:
            padded = jnp.zeros((2, beam_rows, grid_size), jnp.float32)
            padded = lax.dynamic_update_slice(
                padded, input_beam, (zero_index, zero_index, offsets[1])
            )
            columns = to_columns(
                transform_last(padded, -1.0), move_window, devices_total, col_count
            )
            spectral = jnp.zeros((2, col_count, grid_size), jnp.float32)
            spectral = lax.dynamic_update_slice(
                spectral, columns, (zero_index, zero_index, offsets[0])
            )
        else:
            spectral = to_columns(
                transform_last(beam_field, -1.0), move_grid, devices_total, col_count
            )
        spectrum = transform_last(spectral, -1.0)
        phases = squared * (distances[layer_index] * phase_coef)
        spectrum = rotate_planes(spectrum, -phases)
        mixed = transform_last(spectrum, 1.0) * scaling
        if layer_index < step_total - 1:
            row_planes = to_rows(mixed, move_grid, devices_total)
            beam_field = transform_last(row_planes, 1.0) * scaling
            screen_phase = block_scales(
                screen_scales[layer_index], position * grid_rows, grid_rows
            ) * screens[layer_index].astype(jnp.float32)
            beam_field = rotate_planes(beam_field, screen_phase)
        else:
            cropped = mixed[:, :, crop_start : crop_start + window_size]
            row_planes = to_rows(cropped, move_window, devices_total)
            beam_field = transform_last(row_planes, 1.0) * scaling
            beam_field = beam_field[:, :, crop_start : crop_start + window_size]
            out_rows = beam_field.shape[1]
            last_phase = block_scales(
                last_scales, position * out_rows, out_rows
            ) * last_screen.astype(jnp.float32)
            beam_field = rotate_planes(beam_field, last_phase)
    return beam_field


def solution(mesh):
    return jax.shard_map(
        body,
        mesh=mesh,
        in_specs=(
            P(None, ("gx", "gy"), None),
            P(),
            P(),
            P(None, ("gx", "gy"), None),
            P(),
            P(("gx", "gy"), None),
            P(),
        ),
        out_specs=P(None, ("gx", "gy"), None),
        check_vma=False,
    )
```

profile of v0, /device:TPU:0, one launch (start us, length us, event | category | flops | bytes accessed | tf_op | source)
XLA Modules:
  0.0 2737.4 jit_solution(1969219986650630541)
XLA Ops:
  7.6 22.6 dynamic_update_slice.6
  124.7 180.9 %all-to-all-done = f32[2,32,32768]{2,0,1:T(2,128)} async-done(((f32[2,32,32768]{2,0,1:T(2,128)}), f32[2,32,32768]{2,0,1:T(2,128)}, u32[]{:S(2)}, u32[]{:S(2)}) %all-to-all-start) | async-done | bytes 8388640 | tf_op jit(solution)/shard_map/all_to_all | solution.py:56
  343.1 44.3 %dynamic_update_slice.7 = f32[2,256,8192]{2,1,0:T(8,128)} dynamic-update-slice(f32[2,256,8192]{2,1,0:T(8,128)} %broadcast_in_dim.8, f32[2,256,4096]{2,1,0:T(8,128)} %copy.195, s32[]{:T(128)} %constant.149.clone.1, s32[]{:T(128)} %constant.149.clone.1, s32[]{:T(128)S(6)} %select_n.300) | dynamic-update-slice | bytes 16777220 | tf_op jit(solution)/shard_map/dynamic_update_slice | solution.py:133
  437.2 19.9 subtract_bitcast_fusion.11
  516.4 19.7 add_bitcast_fusion.10
  544.4 35.6 %fusion.5 = (f32[256,64,128]{0,2,1:T(8,128)}, f32[256,64,128]{0,2,1:T(8,128)}) fusion(f32[]{:T(128)} %bitcast.20, s32[64,128]{1,0:T(8,128)S(1)} %fusion.165, s32[256]{0:T(256)S(1)} %get-tuple-element.48, f32[256,64,128]{0,2,1:T(8,128)S(1)} %bitcast.435, f32[256,64,128]{0,2,1:T(8,128)S(1)} %bitcast.432), kind=kLoop, calls=%fused_computation.23 | loop fusion | flops 20971520 | bytes 33588228 | tf_op jit(solution)/shard_map/add | solution.py:97
  632.5 19.6 subtract_bitcast_fusion.9
  652.2 18.5 fusion.46
  683.7 19.2 subtract_bitcast_fusion.8
  764.2 27.3 reshape.306
  805.0 355.5 %all-to-all-done.1 = f32[2,32,65536]{2,0,1:T(2,128)} async-done(((f32[2,32,65536]{2,0,1:T(2,128)}), f32[2,32,65536]{2,0,1:T(2,128)}, u32[]{:S(2)}, u32[]{:S(2)}) %all-to-all-start.1) | async-done | bytes 16777248 | tf_op jit(solution)/shard_map/all_to_all | solution.py:60
  1160.5 28.9 %reshape.307 = f32[2,32,256,256]{3,2,0,1:T(8,128)} reshape(f32[2,32,65536]{2,0,1:T(2,128)} %all-to-all-done.1) | data formatting | bytes 33554432 | tf_op jit(solution)/shard_map/reshape | solution.py:76
  1254.9 19.8 subtract_bitcast_fusion.7
  1274.8 18.5 fusion.38
  1306.0 19.3 subtract_bitcast_fusion.6
  1336.9 17.9 add_bitcast_fusion.6
  1396.6 34.9 %multiply_add_fusion = (f32[256,64,128]{2,1,0:T(8,128)S(1)}, f32[256,64,128]{2,1,0:T(8,128)S(1)}) fusion(f32[256,64,128]{2,1,0:T(8,128)} %copy.225, f32[256,64,128]{2,1,0:T(8,128)} %copy.224, f32[32,8,64,128]{3,2,1,0:T(8,128)} %copy.283, f32[256,64]{1,0:T(8,128)S(1)} %fusion.110), kind=kLoop, calls=%fused_computation.39 | loop fusion | flops 14680064 | bytes 42008576 | tf_op jit(solution)/shard_map/add | solution.py:97
  1461.3 19.6 subtract_bitcast_fusion.5
  1481.0 18.5 fusion.30
  1512.5 19.2 subtract_bitcast_fusion.4
  1543.3 17.9 add_bitcast_fusion.4
  1590.3 28.6 %copy.234 = f32[2,32,65536]{2,0,1:T(2,128)} copy(f32[2,32,65536]{2,1,0:T(8,128)} %reshape.293) | data formatting | bytes 33554432 | tf_op jit(solution)/shard_map/reshape | solution.py:66
  1623.5 364.0 %all-to-all-done.2 = f32[2,32,65536]{2,0,1:T(2,128)} async-done(((f32[2,32,65536]{2,0,1:T(2,128)}), f32[2,32,65536]{2,0,1:T(2,128)}, u32[]{:S(2)}, u32[]{:S(2)}) %all-to-all-start.2) | async-done | bytes 16777248 | tf_op jit(solution)/shard_map/all_to_all | solution.py:60
  1987.5 28.9 %reshape.308 = f32[2,32,256,256]{3,2,0,1:T(8,128)} reshape(f32[2,32,65536]{2,0,1:T(2,128)} %all-to-all-done.2) | data formatting | bytes 33554432 | tf_op jit(solution)/shard_map/reshape | solution.py:67
  2102.2 19.4 subtract_bitcast_fusion.3
  2181.5 19.7 add_bitcast_fusion.2
  2209.5 35.6 %fusion.3 = (f32[256,64,128]{0,2,1:T(8,128)}, f32[256,64,128]{0,2,1:T(8,128)}) fusion(f32[]{:T(128)} %bitcast.56, s32[64,128]{1,0:T(8,128)S(1)} %copy-done.25, s32[256]{0:T(256)S(1)} %copy-done.27, f32[256,64,128]{0,2,1:T(8,128)S(1)} %bitcast.433, f32[256,64,128]{0,2,1:T(8,128)S(1)} %bitcast.431), kind=kLoop, calls=%fused_computation.17 | loop fusion | flops 20971520 | bytes 33588228 | tf_op jit(solution)/shard_map/add | solution.py:97
  2297.7 19.6 subtract_bitcast_fusion.1
  2317.3 18.5 fusion.14
  2348.8 19.2 subtract_bitcast_fusion
  2379.6 17.9 add_bitcast_fusion
  2449.6 182.7 %all-to-all-done.3 = f32[2,32,32768]{2,0,1:T(2,128)} async-done(((f32[2,32,32768]{2,0,1:T(2,128)}), f32[2,32,32768]{2,0,1:T(2,128)}, u32[]{:S(2)}, u32[]{:S(2)}) %all-to-all-start.3) | async-done | bytes 8388640 | tf_op jit(solution)/shard_map/all_to_all | solution.py:56
  (223 shorter events, 999.4 us)
Async XLA Ops:
  0.0 804.8 %copy-start = (f32[1,64,64]{2,1,0:T(8,128)S(1)}, f32[1,64,64]{2,1,0:T(8,128)}, u32[]{:S(2)}) copy-start(f32[1,64,64]{2,1,0:T(8,128)} %param.11) | copy-start | bytes 49156
  43.5 393.7 %copy-start.22 = (f32[64,128]{1,0:T(8,128)}, f32[64,128]{1,0:T(8,128)S(1)}, u32[]{:S(2)}) copy-start(f32[64,128]{1,0:T(8,128)S(1)} %get-tuple-element.45) | copy-start | bytes 98308
  113.2 192.3 %all-to-all-start = ((f32[2,32,32768]{2,0,1:T(2,128)}), f32[2,32,32768]{2,0,1:T(2,128)}, u32[]{:S(2)}, u32[]{:S(2)}) async-start(f32[2,32,32768]{2,0,1:T(2,128)} %copy.192), calls=%async_computation | async-start | bytes 16777216 | tf_op jit(solution)/shard_map/all_to_all | solution.py:56
  124.5 419.9 %copy-start.26 = (s32[256]{0:T(256)}, s32[256]{0:T(256)S(1)}, u32[]{:S(2)}) copy-start(s32[256]{0:T(256)S(1)} %get-tuple-element.48) | copy-start | bytes 3076
  124.5 419.9 %copy-start.24 = (s32[64,128]{1,0:T(8,128)}, s32[64,128]{1,0:T(8,128)S(1)}, u32[]{:S(2)}) copy-start(s32[64,128]{1,0:T(8,128)S(1)} %fusion.165) | copy-start | bytes 98308
  124.7 1130.3 %copy-start.20 = (f32[64,128]{1,0:T(8,128)}, f32[64,128]{1,0:T(8,128)S(1)}, u32[]{:S(2)}) copy-start(f32[64,128]{1,0:T(8,128)S(1)} %fusion.284) | copy-start | bytes 98308
  457.1 16.2 copy-start.8
  457.1 33.3 %slice-start.2 = ((s8[8388608]{0:T(1024)(128)(4,1)}), s8[4194304]{0:T(1024)(128)(4,1)S(1)}, s32[]{:S(2)}) async-start(s8[8388608]{0:T(1024)(128)(4,1)} %bitcast.411), calls=%async_computation.6 | async-start | bytes 8388608
  473.3 17.1 slice-start.3
  588.7 13.0 copy-start.3
  652.1 18.6 copy-start.9
  652.2 31.5 %slice-start.4 = ((s8[8388608]{0:T(1024)(128)(4,1)}), s8[4194304]{0:T(1024)(128)(4,1)S(1)}, s32[]{:S(2)}) async-start(s8[8388608]{0:T(1024)(128)(4,1)} %bitcast.413), calls=%async_computation.8 | async-start | bytes 8388608
  670.7 13.0 slice-start.5
  791.5 369.0 %all-to-all-start.1 = ((f32[2,32,65536]{2,0,1:T(2,128)}), f32[2,32,65536]{2,0,1:T(2,128)}, u32[]{:S(2)}, u32[]{:S(2)}) async-start(f32[2,32,65536]{2,0,1:T(2,128)} %reshape.306), calls=%async_computation.1 | async-start | bytes 33554432 | tf_op jit(solution)/shard_map/all_to_all | solution.py:60
  1211.3 13.0 copy-start.4
  1274.8 18.5 copy-start.10
  1274.8 31.3 %slice-start.6 = ((s8[8388608]{0:T(1024)(128)(4,1)}), s8[4194304]{0:T(1024)(128)(4,1)S(1)}, s32[]{:S(2)}) async-start(s8[8388608]{0:T(1024)(128)(4,1)} %bitcast.415), calls=%async_computation.10 | async-start | bytes 8388608
  1431.5 20.1 copy-start.2
  1481.0 18.6 copy-start.11
  1481.0 31.5 %slice-start.8 = ((s8[8388608]{0:T(1024)(128)(4,1)}), s8[4194304]{0:T(1024)(128)(4,1)S(1)}, s32[]{:S(2)}) async-start(s8[8388608]{0:T(1024)(128)(4,1)} %bitcast.417), calls=%async_computation.12 | async-start | bytes 8388608
  1499.5 13.0 slice-start.9
  1618.8 368.7 %all-to-all-start.2 = ((f32[2,32,65536]{2,0,1:T(2,128)}), f32[2,32,65536]{2,0,1:T(2,128)}, u32[]{:S(2)}, u32[]{:S(2)}) async-start(f32[2,32,65536]{2,0,1:T(2,128)} %copy.234), calls=%async_computation.2 | async-start | bytes 33554432 | tf_op jit(solution)/shard_map/all_to_all | solution.py:60
  2050.0 13.1 copy-start.5
  2050.0 23.1 slice-start.12
  2121.7 16.7 copy-start.7
  2121.7 33.8 %slice-start = ((s8[8388608]{0:T(1024)(128)(4,1)}), s8[4194304]{0:T(1024)(128)(4,1)S(1)}, s32[]{:S(2)}) async-start(s8[8388608]{0:T(1024)(128)(4,1)} %bitcast.409), calls=%async_computation.4 | async-start | bytes 8388608
  2138.4 17.1 slice-start.1
  2253.9 13.0 copy-start.6
  2317.3 18.6 copy-start.12
  2317.3 31.5 %slice-start.10 = ((s8[8388608]{0:T(1024)(128)(4,1)}), s8[4194304]{0:T(1024)(128)(4,1)S(1)}, s32[]{:S(2)}) async-start(s8[8388608]{0:T(1024)(128)(4,1)} %bitcast.419), calls=%async_computation.14 | async-start | bytes 8388608
  2335.8 13.0 slice-start.11
  2443.5 188.9 %all-to-all-start.3 = ((f32[2,32,32768]{2,0,1:T(2,128)}), f32[2,32,32768]{2,0,1:T(2,128)}, u32[]{:S(2)}, u32[]{:S(2)}) async-start(f32[2,32,32768]{2,0,1:T(2,128)} %copy.255), calls=%async_computation.3 | async-start | bytes 16777216 | tf_op jit(solution)/shard_map/all_to_all | solution.py:56
  (17 other events, 141.9 us)
where the time goes:
time: 2750 us; the launch traced here: 2740 us
  waiting for transfers between devices  1080 us (39%)
  matrix products  830 us (30%)
  local copies, waits for them, and re-layouts  650 us (24%)
  other arithmetic  148 us (5%)
    dot_general x64, matrix products, contract(): jnp.einsum(pattern, lhs_array, rhs_array, precision=lax.Precision.HIGHEST...  829 us
    all_to_all x2, waiting for transfers between devices, move_grid(): lax.all_to_all(blocks, ('gx', 'gy'), split_axis=1, concat_axis=1, tiled=T...  720 us
    all_to_all x2, waiting for transfers between devices, move_window(): lax.all_to_all(blocks, ('gx', 'gy'), split_axis=1, concat_axis=1, tiled=T...  364 us
    add x3, other arithmetic, rotate_planes(): planes[0] * sine + planes[1] * cosine  106 us
    reshape x4, local copies, waits for them, and re-layouts, to_rows(): arrived = mover(blocks.reshape((2, devices_total, col_count * row_count)))  69.5 us
    reshape x4, local copies, waits for them, and re-layouts, to_columns(): arrived = mover(blocks.reshape((2, devices_total, col_count * row_count)))  67.9 us
    sub x8, local copies, waits for them, and re-layouts, transform_last(): contract('bkq,qm->bmk', second_real, cos_inner)  67.8 us
    add x8, local copies, waits for them, and re-layouts, transform_last(): contract('bkq,qm->bmk', second_real, sin_inner)  58.4 us
  transfers between devices with their start and end apart: 4, of which 4 were waited for; matrix products, arithmetic and copies ran while one was open for 0% of the time, Pallas kernels for 0%

commit v1 on v0

v1 whole, which is shorter than its diff:
```python
import math

import jax
import jax.numpy as jnp
from jax import lax
from jax.experimental import pallas as pl
from jax.experimental.pallas import tpu as pltpu
from jax.sharding import PartitionSpec as P

AXES = ("gx", "gy")
INNER = 128


def contract(pattern, lhs_array, rhs_array, precision=lax.Precision.HIGH):
    return jnp.einsum(
        pattern, lhs_array, rhs_array, precision=precision, preferred_element_type=jnp.float32
    )


def unit_angles(product, length):
    angles = (product % length).astype(jnp.float32) * (2.0 * math.pi / length)
    return jnp.cos(angles), jnp.sin(angles)


def operator_lags(distance, shift, length):
    outer = length // INNER
    k_ids = jnp.arange(outer, dtype=jnp.int32)
    m_ids = jnp.arange(INNER, dtype=jnp.int32)
    index = k_ids[:, None] + outer * m_ids[None, :]
    signed = jnp.where(index < length // 2, index, index - length)
    phases = (signed * signed).astype(jnp.float32) * (
        distance * ((2.0 * math.pi / length) ** 2)
    )
    phase_re, phase_im = jnp.cos(phases), -jnp.sin(phases)
    shift_re, shift_im = unit_angles(index * shift, length)
    filt_re = phase_re * shift_re - phase_im * shift_im
    filt_im = phase_re * shift_im + phase_im * shift_re
    lag_ids = jnp.arange(2 * INNER, dtype=jnp.int32)
    lags = jnp.where(lag_ids < INNER, lag_ids, lag_ids - 2 * INNER)
    table_re, table_im = unit_angles(m_ids[:, None] * lags[None, :], INNER)
    best = lax.Precision.HIGHEST
    sum_re = contract("km,md->kd", filt_re, table_re, best) - contract(
        "km,md->kd", filt_im, table_im, best
    )
    sum_im = contract("km,md->kd", filt_re, table_im, best) + contract(
        "km,md->kd", filt_im, table_re, best
    )
    twist_re, twist_im = unit_angles(k_ids[:, None] * lags[None, :], length)
    scale = 1.0 / length
    return (
        (sum_re * twist_re - sum_im * twist_im) * scale,
        (sum_re * twist_im + sum_im * twist_re) * scale,
    )


def toeplitz_kernel(lag_re_ref, lag_im_ref, out_ref):
    for slot in range(lag_re_ref.shape[0]):
        parts = []
        for lag_ref in (lag_re_ref, lag_im_ref):
            wide = jnp.broadcast_to(lag_ref[slot, :][None, :], (INNER, 2 * INNER))
            parts.append(pltpu.roll(wide, 0, 1, stride=1, stride_axis=0)[:, :INNER])
        out_ref[slot, :INNER, :INNER] = parts[0]
        out_ref[slot, :INNER, INNER:] = parts[1]
        out_ref[slot, INNER:, :INNER] = -parts[1]
        out_ref[slot, INNER:, INNER:] = parts[0]


def toeplitz(lag_re, lag_im):
    outer = lag_re.shape[0]
    block = 8
    return pl.pallas_call(
        toeplitz_kernel,
        grid=(outer // block,),
        in_specs=[pl.BlockSpec((block, 2 * INNER), lambda step: (step, 0))] * 2,
        out_specs=pl.BlockSpec((block, 2 * INNER, 2 * INNER), lambda step: (step, 0, 0)),
        out_shape=jax.ShapeDtypeStruct((outer, 2 * INNER, 2 * INNER), jnp.float32),
    )(lag_re, lag_im)


def embed(real_part, imag_part, axis_in, axis_out):
    top = jnp.stack([real_part, imag_part], axis=axis_out)
    low = jnp.stack([-imag_part, real_part], axis=axis_out)
    return jnp.stack([top, low], axis=axis_in)


def propagate(planes, distance, shift, length, out_outer):
    outer = length // INNER
    in_outer = planes.shape[2]
    ids = jnp.arange(outer, dtype=jnp.int32)
    dft_re, dft_im = unit_angles(ids[:, None] * ids[None, :], outer)
    first = embed(dft_re[:in_outer], -dft_im[:in_outer], 0, 1)
    last = embed(dft_re[:, :out_outer], dft_im[:, :out_outer], 0, 1)
    lag_re, lag_im = operator_lags(distance, shift, length)
    middle = toeplitz(lag_re, lag_im).reshape((outer, 2, INNER, 2, INNER))
    spectral = contract("cbpq,cpdk->kbdq", planes, first)
    mixed = contract("kbdq,kdqes->kbes", spectral, middle)
    return contract("kbes,ekfp->fbps", mixed, last)


def move(blocks):
    return lax.all_to_all(blocks, AXES, split_axis=1, concat_axis=1, tiled=True)


def to_columns(planes, devices_total):
    count, row_count, width = planes.shape
    col_count = width // devices_total
    blocks = planes.reshape((count, row_count, devices_total, col_count)).transpose((0, 2, 3, 1))
    arrived = move(blocks.reshape((count, devices_total, col_count * row_count)))
    arrived = arrived.reshape((count, devices_total, col_count, row_count)).transpose((0, 2, 1, 3))
    return arrived.reshape((count, col_count, devices_total * row_count))


def to_rows(planes, devices_total):
    count, col_count, height = planes.shape
    row_count = height // devices_total
    blocks = planes.reshape((count, col_count, devices_total, row_count)).transpose((0, 2, 1, 3))
    arrived = move(blocks.reshape((count, devices_total, col_count * row_count)))
    arrived = arrived.reshape((count, devices_total, col_count, row_count)).transpose((0, 3, 1, 2))
    return arrived.reshape((count, row_count, devices_total * col_count))


def pick_scales(scales, first, count):
    block_ids = (first + jnp.arange(count, dtype=jnp.int32)) // 128
    onehot = (
        block_ids[:, None] == jnp.arange(scales.shape[0], dtype=jnp.int32)[None, :]
    ).astype(jnp.float32)
    return jnp.dot(
        onehot, scales, precision=lax.Precision.HIGHEST, preferred_element_type=jnp.float32
    )


def rotate_planes(planes, phases):
    cosine = jnp.cos(phases)
    sine = jnp.sin(phases)
    return jnp.stack([planes[0] * cosine - planes[1] * sine, planes[0] * sine + planes[1] * cosine])


def body(input_beam, offsets, distances, screens, screen_scales, last_screen, last_scales):
    devices_total = lax.axis_size(AXES)
    position = lax.axis_index(AXES)
    length = screens.shape[2]
    window = input_beam.shape[2]
    rows = input_beam.shape[1]
    outer = length // INNER
    window_outer = window // INNER
    cols = length // devices_total
    steps = distances.shape[0]
    crop = (length - window) // 2
    flat_screens = [to_columns(screens[s : s + 1], devices_total)[0] for s in range(steps - 1)]
    field = propagate(
        input_beam.reshape((2, rows, window_outer, INNER)), distances[0], -offsets[1], length, outer
    )
    field = to_columns(field.reshape((2, rows, length)), devices_total)
    field = field.reshape((2, cols, window_outer, INNER))
    for step in range(steps):
        final = step == steps - 1
        shift = jnp.zeros((), jnp.int32)
        if step == 0:
            shift = shift - offsets[0]
        if final:
            shift = shift + crop
        field = propagate(
            field, distances[step], shift, length, window_outer if final else outer
        )
        if not final:
            phases = pick_scales(screen_scales[step].T, position * cols, cols)[
                :, :, None
            ] * flat_screens[step].reshape((cols, outer, INNER)).astype(jnp.float32)
            field = rotate_planes(field, phases)
    field = to_rows(field.reshape((2, cols, window)), devices_total)
    field = propagate(
        field.reshape((2, rows, outer, INNER)),
        distances[steps - 1],
        jnp.full((), crop, jnp.int32),
        length,
        window_outer,
    )
    phases = pick_scales(last_scales, position * rows, rows)[:, :, None] * last_screen.reshape(
        (rows, window_outer, INNER)
    ).astype(jnp.float32)
    return rotate_planes(field, phases).reshape((2, rows, window))


def solution(mesh):
    return jax.shard_map(
        body,
        mesh=mesh,
        in_specs=(
            P(None, AXES, None),
            P(),
            P(),
            P(None, AXES, None),
            P(),
            P(AXES, None),
            P(),
        ),
        out_specs=P(None, AXES, None),
        check_vma=False,
    )
```

time: 2750 us -> 975 us (0.35)
  waiting for transfers between devices: 1080 us -> 360 us
  matrix products: 830 us -> 253 us
  local copies, waits for them, and re-layouts: 650 us -> 225 us
  other arithmetic: 148 us -> 77.3 us
  Pallas kernels: 0 us -> 28 us
    all_to_all x4 -> x3, waiting for transfers between devices: 1080 us -> 360 us  [move(): return lax.all_to_all(blocks, AXES, split_axis=1, concat_axis=1, tiled=True)]
    dot_general x66 -> x26, matrix products: 830 us -> 253 us  [the longest x24 253 us: contract(): jnp.einsum(pattern, lhs_array, rhs_array, precision=precision, preferred_...]
    add x3 -> x0, other arithmetic: 106 us -> none  [rotate_planes(): planes[0] * sine + planes[1] * cosine]
    sub x10 -> x0, local copies, waits for them, and re-layouts: 85.3 us -> none  [the longest x8 67.8 us: transform_last(): contract('bkq,qm->bmk', second_real, cos_inner)]
    reshape x17 -> x12, local copies, waits for them, and re-layouts: 254 us -> 171 us  [the longest x3 62.4 us: propagate(): middle = toeplitz(lag_re, lag_im).reshape((outer, 2, INNER, 2, INNER))]
    add x10 -> x0, local copies, waits for them, and re-layouts: 76 us -> none  [the longest x8 58.4 us: transform_last(): contract('bkq,qm->bmk', second_real, sin_inner)]
    dynamic_update_slice x2 -> x0, local copies, waits for them, and re-layouts: 66.9 us -> none  [the longest x1 44.3 us: body(): lax.dynamic_update_slice(spectral, columns, (zero_index, zero_index, offs...]
    squeeze x8 -> x0, local copies, waits for them, and re-layouts: 63.8 us -> none  [the longest x3 23.2 us: transform_last(): imag_part = grouped[1]]
  transfers between devices with their start and end apart: 4 -> 3, of which waited for: 4 -> 3; matrix products, arithmetic and copies ran while one was open for 0% -> 18% of each run, Pallas kernels for 0% -> 2%
where the time goes in v1:
time: 975 us; the launch traced here: 962 us
  waiting for transfers between devices  360 us (37%)
  matrix products  253 us (26%)
  local copies, waits for them, and re-layouts  225 us (23%)
  other arithmetic  77.3 us (8%)
  Pallas kernels  28 us (3%)
  starting transfers between devices  15.5 us (2%)
    all_to_all x3, waiting for transfers between devices, move(): return lax.all_to_all(blocks, AXES, split_axis=1, concat_axis=1, tiled=True)  360 us
    dot_general x24, matrix products, contract(): jnp.einsum(pattern, lhs_array, rhs_array, precision=precision, preferred_...  253 us
    reshape x3, local copies, waits for them, and re-layouts, propagate(): middle = toeplitz(lag_re, lag_im).reshape((outer, 2, INNER, 2, INNER))  62.4 us
    reshape x3, local copies, waits for them, and re-layouts, to_columns(): blocks.reshape((count, devices_total, col_count * row_count))  47.4 us
    sub x2, other arithmetic, rotate_planes(): planes[0] * cosine - planes[1] * sine  44.8 us
    pallas_call x3, Pallas kernels, toeplitz(): pl.pallas_call(toeplitz_kernel, grid=(outer // block,), in_specs=[pl.Bloc...  28 us
    convert_element_type x1, other arithmetic, body(): flat_screens[step].reshape((cols, outer, INNER)).astype(jnp.float32)  27 us
    reshape x2, local copies, waits for them, and re-layouts, to_rows(): arrived.reshape((count, devices_total, col_count, row_count))  22.1 us
  transfers between devices with their start and end apart: 3, of which 3 were waited for; matrix products, arithmetic and copies ran while one was open for 18% of the time, Pallas kernels for 2%

profile of v1, /device:TPU:0, one launch (start us, length us, event | category | flops | bytes accessed | tf_op | source)
XLA Modules:
  0.0 962.0 jit_solution(18419639762333067235)
XLA Ops:
  18.3 9.5 shard_map.73
  27.8 20.8 %reshape.227 = f32[64,2,128,2,128]{4,3,2,1,0:T(2,128)} reshape(f32[64,256,256]{2,1,0:T(8,128)} %shard_map.73) | data formatting | bytes 33554432 | tf_op jit(solution)/shard_map/reshape | solution.py:94
  57.2 21.5 %fusion.57 = f32[64,128,2,128]{3,1,2,0:T(8,128)S(1)} fusion(f32[64,2,128,2,128]{4,3,2,1,0:T(2,128)} %reshape.227, f32[64,128,2,128,1]{3,0,1,2,4:T(8,128)} %fusion.65), kind=kOutput, calls=%fused_computation.47 | convolution fusion | flops 3221225472 | bytes 33554432 | tf_op jit(solution)/shard_map/kbdq,kdqes->kbes/dot_general | solution.py:15
  78.8 13.8 %fusion.62 = f32[2,128,64,128]{3,2,1,0:T(8,128)} fusion(f32[64,128,2,128]{3,1,2,0:T(8,128)S(1)} %fusion.57, f32[1,64,2,64]{1,3,0,2:T(8,128)S(1)} %get-tuple-element.16, f32[1,64,2,64]{1,3,0,2:T(8,128)S(1)} %get-tuple-element.23), kind=kOutput, calls=%fused_computation.48 | convolution fusion | flops 1610629120 | bytes 16842752 | tf_op jit(solution)/shard_map/kbes,ekfp->fbps/dot_general | solution.py:15
  101.4 9.4 reshape.228
  110.8 15.4 %copy.57 = f32[2,32,32768]{2,0,1:T(2,128)} copy(f32[2,32,32768]{2,1,0:T(8,128)} %reshape.228) | data formatting | bytes 16777216 | tf_op jit(solution)/shard_map/reshape | solution.py:108
  133.6 9.0 copy.121
  142.6 22.7 %reshape.267 = s32[1,32,65536]{2,0,1:T(1,128)} reshape(s32[1,32,256,256]{3,2,1,0:T(8,128)} %bitcast.230) | data formatting | bytes 16777216 | tf_op jit(solution)/shard_map/reshape | solution.py:108
  165.3 153.2 %all-to-all-done = f32[2,32,32768]{2,0,1:T(2,128)} async-done(((f32[2,32,32768]{2,0,1:T(2,128)}), f32[2,32,32768]{2,0,1:T(2,128)}, u32[]{:S(2)}, u32[]{:S(2)}) %all-to-all-start) | async-done | bytes 8388640 | tf_op jit(solution)/shard_map/all_to_all | solution.py:101
  322.6 9.3 shard_map.74
  331.9 20.8 %reshape.230 = f32[64,2,128,2,128]{4,3,2,1,0:T(2,128)} reshape(f32[64,256,256]{2,1,0:T(8,128)} %shard_map.74) | data formatting | bytes 33554432 | tf_op jit(solution)/shard_map/reshape | solution.py:94
  352.7 9.3 shard_map.75
  362.0 20.8 %reshape.233 = f32[64,2,128,2,128]{4,3,2,1,0:T(2,128)} reshape(f32[64,256,256]{2,1,0:T(8,128)} %shard_map.75) | data formatting | bytes 33554432 | tf_op jit(solution)/shard_map/reshape | solution.py:94
  383.1 11.8 %reshape.266 = f32[2,32,256,128]{3,2,0,1:T(8,128)} reshape(f32[2,32,32768]{2,0,1:T(2,128)} %all-to-all-done) | data formatting | bytes 16777216 | tf_op jit(solution)/shard_map/reshape | solution.py:109
  394.9 23.2 %fusion.40 = f32[64,256,2,128,1]{3,0,1,2,4:T(8,128)} fusion(f32[2,32,256,128]{3,2,0,1:T(8,128)} %reshape.266, f32[1,32,2,64]{3,1,0,2:T(8,128)S(1)} %get-tuple-element.28, f32[1,32,2,64]{3,1,0,2:T(8,128)S(1)} %get-tuple-element.27), kind=kOutput, calls=%fused_computation.39 | convolution fusion | flops 1610620928 | bytes 25198592 | tf_op jit(solution)/shard_map/cbpq,cpdk->kbdq/dot_general | solution.py:15
  418.1 39.3 %fusion.19 = f32[64,256,2,128]{3,1,2,0:T(8,128)} fusion(f32[64,2,128,2,128]{4,3,2,1,0:T(2,128)} %reshape.230, f32[64,256,2,128,1]{3,0,1,2,4:T(8,128)} %fusion.40), kind=kOutput, calls=%fused_computation.20 | convolution fusion | flops 6442450944 | bytes 50331648 | tf_op jit(solution)/shard_map/kbdq,kdqes->kbes/dot_general | solution.py:15
  457.4 25.7 %fusion.43 = f32[2,256,64,128]{3,2,1,0:T(8,128)} fusion(f32[64,256,2,128]{3,1,2,0:T(8,128)} %fusion.19, f32[1,64,2,64]{1,3,0,2:T(8,128)S(1)} %get-tuple-element.16, f32[1,64,2,64]{1,3,0,2:T(8,128)S(1)} %get-tuple-element.23), kind=kOutput, calls=%fused_computation.40 | convolution fusion | flops 3221241856 | bytes 33619968 | tf_op jit(solution)/shard_map/kbes,ekfp->fbps/dot_general | solution.py:15
  483.0 24.5 %all-to-all-done.1 = s32[1,32,65536]{2,0,1:T(1,128)} async-done(((s32[1,32,65536]{2,0,1:T(1,128)}), s32[1,32,65536]{2,0,1:T(1,128)}, u32[]{:S(2)}, u32[]{:S(2)}) %all-to-all-start.1) | async-done | bytes 8388640 | tf_op jit(solution)/shard_map/all_to_all | solution.py:101
  507.5 27.0 %convert_reduce_fusion = f32[32,65536]{1,0:T(8,128)} fusion(s32[1,32,65536]{2,0,1:T(1,128)} %all-to-all-done.1), kind=kLoop, calls=%fused_computation.36 | loop fusion | flops 2097152 | bytes 16777216 | tf_op jit(solution)/shard_map/convert_element_type | solution.py:168
  549.4 8.9 convert_element_type.184
  558.3 35.8 %multiply_subtract_fusion = (f32[1,256,64,128]{3,2,1,0:T(8,128)S(1)}, f32[1,256,64,128]{3,2,1,0:T(8,128)}) fusion(f32[2,256,64,128]{3,2,1,0:T(8,128)} %fusion.43, f32[1,256,64,128]{3,2,1,0:T(8,128)} %convert_element_type.184, f32[256,64]{1,0:T(8,128)S(1)} %fusion.82), kind=kLoop, calls=%fused_computation.35 | loop fusion | flops 14680064 | bytes 42008576 | tf_op jit(solution)/shard_map/sub | solution.py:135
  594.1 13.3 %fusion.46 = f32[64,256,2,128,1]{3,0,1,2,4:T(8,128)} fusion(f32[1,256,64,128]{3,2,1,0:T(8,128)} %get-tuple-element.6, f32[1,256,64,128]{3,2,1,0:T(8,128)S(1)} %get-tuple-element.5, f32[1,64,2,64]{1,3,2,0:T(8,128)S(1)} %get-tuple-element.24, f32[1,64,2,64]{1,3,2,0:T(8,128)S(1)} %get-tuple-element.15), kind=kOutput, calls=%fused_computation.41 | convolution fusion | flops 3225436160 | bytes 33619968 | tf_op jit(solution)/shard_map/cbpq,cpdk->kbdq/dot_general | solution.py:15
  607.4 39.1 %fusion.24 = f32[64,256,2,128]{3,1,2,0:T(8,128)} fusion(f32[64,2,128,2,128]{4,3,2,1,0:T(2,128)} %reshape.233, f32[64,256,2,128,1]{3,0,1,2,4:T(8,128)} %fusion.46), kind=kOutput, calls=%fused_computation.21 | convolution fusion | flops 6442450944 | bytes 50331648 | tf_op jit(solution)/shard_map/kbdq,kdqes->kbes/dot_general | solution.py:15
  646.6 21.6 %fusion.68 = f32[2,32,256,128]{3,1,2,0:T(8,128)S(1)} fusion(f32[64,256,2,128]{3,1,2,0:T(8,128)} %fusion.24, f32[1,64,2,32]{3,1,2,0:T(8,128)S(1)} %get-tuple-element.20, f32[1,64,2,32]{3,1,2,0:T(8,128)S(1)} %get-tuple-element.19), kind=kOutput, calls=%fused_computation.51 | convolution fusion | flops 1610620928 | bytes 25198592 | tf_op jit(solution)/shard_map/kbes,ekfp->fbps/dot_general | solution.py:15
  676.3 10.6 %reshape.268 = f32[2,32,32768]{2,0,1:T(2,128)} reshape(f32[2,32,256,128]{3,2,0,1:T(8,128)} %copy.124) | data formatting | bytes 16777216 | tf_op jit(solution)/shard_map/reshape | solution.py:117
  693.0 182.7 %all-to-all-done.2 = f32[2,32,32768]{2,0,1:T(2,128)} async-done(((f32[2,32,32768]{2,0,1:T(2,128)}), f32[2,32,32768]{2,0,1:T(2,128)}, u32[]{:S(2)}, u32[]{:S(2)}) %all-to-all-start.2) | async-done | bytes 8388640 | tf_op jit(solution)/shard_map/all_to_all | solution.py:101
  875.7 11.8 %reshape.235 = f32[2,32,256,128]{3,2,0,1:T(8,128)} reshape(f32[2,32,32768]{2,0,1:T(2,128)} %all-to-all-done.2) | data formatting | bytes 16777216 | tf_op jit(solution)/shard_map/reshape | solution.py:118
  887.5 10.3 %copy.75 = f32[2,32,256,128]{2,1,0,3:T(8,128)} copy(f32[2,32,256,128]{3,2,0,1:T(8,128)} %reshape.235) | data formatting | bytes 16777216 | tf_op jit(solution)/shard_map/reshape | solution.py:118
  897.8 8.9 reshape.259
  913.1 19.4 %fusion.52 = f32[64,128,2,128]{3,1,2,0:T(8,128)} fusion(f32[64,2,128,2,128]{4,3,2,1,0:T(2,128)} %reshape.233, f32[64,128,2,128,1]{3,0,1,2,4:T(8,128)S(1)} %convolution_bitcast_fusion), kind=kOutput, calls=%fused_computation.46 | convolution fusion | flops 3221225472 | bytes 33554432 | tf_op jit(solution)/shard_map/kbdq,kdqes->kbes/dot_general | solution.py:15
  932.6 11.1 %fusion.71 = f32[2,128,32,128]{3,2,1,0:T(8,128)S(1)} fusion(f32[64,128,2,128]{3,1,2,0:T(8,128)} %fusion.52, f32[1,64,2,32]{3,1,2,0:T(8,128)S(1)} %get-tuple-element.20, f32[1,64,2,32]{3,1,2,0:T(8,128)S(1)} %get-tuple-element.19), kind=kOutput, calls=%fused_computation.52 | convolution fusion | flops 805314560 | bytes 12615680 | tf_op jit(solution)/shard_map/kbes,ekfp->fbps/dot_general | solution.py:15
  943.7 9.1 multiply_subtract_fusion.1
  (55 shorter events, 89.4 us)
Async XLA Ops:
  0.0 382.8 %copy-start = (f32[1,64,64]{2,1,0:T(8,128)S(1)}, f32[1,64,64]{2,1,0:T(8,128)}, u32[]{:S(2)}) copy-start(f32[1,64,64]{2,1,0:T(8,128)} %param.11) | copy-start | bytes 49156
  126.1 192.4 %all-to-all-start = ((f32[2,32,32768]{2,0,1:T(2,128)}), f32[2,32,32768]{2,0,1:T(2,128)}, u32[]{:S(2)}, u32[]{:S(2)}) async-start(f32[2,32,32768]{2,0,1:T(2,128)} %copy.57), calls=%async_computation | async-start | bytes 16777216 | tf_op jit(solution)/shard_map/all_to_all | solution.py:101
  318.5 189.0 %all-to-all-start.1 = ((s32[1,32,65536]{2,0,1:T(1,128)}), s32[1,32,65536]{2,0,1:T(1,128)}, u32[]{:S(2)}, u32[]{:S(2)}) async-start(s32[1,32,65536]{2,0,1:T(1,128)} %reshape.267), calls=%async_computation.1 | async-start | bytes 16777216 | tf_op jit(solution)/shard_map/all_to_all | solution.py:101
  686.8 4.0 copy-start.3
  686.8 188.9 %all-to-all-start.2 = ((f32[2,32,32768]{2,0,1:T(2,128)}), f32[2,32,32768]{2,0,1:T(2,128)}, u32[]{:S(2)}, u32[]{:S(2)}) async-start(f32[2,32,32768]{2,0,1:T(2,128)} %reshape.268), calls=%async_computation.2 | async-start | bytes 16777216 | tf_op jit(solution)/shard_map/all_to_all | solution.py:101
  690.8 1.9 copy-start.4
  932.6 11.1 %copy-start.2 = (f32[16,8,32,128]{3,2,1,0:T(8,128)S(1)}, f32[16,8,32,128]{3,2,1,0:T(8,128)}, u32[]{:S(2)}) copy-start(f32[16,8,32,128]{3,2,1,0:T(8,128)} %copy.130) | copy-start | bytes 6291460
  952.8 9.0 copy-start.1
